TPU v7x, 32 devices: a whole 2x2x4 slice. The times are simulated.
32 devices in a mesh: grp: 8 (over z, core), brk: 4 (over y, x).
Axes of the slice: x: 2, y: 2, z: 4, core: 2. Of those that a mesh axis runs over, the one named last changes fastest.
Arguments:
- state: float32 [8, 5, 192, 64, 128], P('grp', None, 'brk'), may hold values from -6 to 6
- adjoint: float32 [8, 5, 192, 64, 128], P('grp', None, 'brk'), may hold values from -6 to 6
- source: float32 [8, 5, 192, 64, 128], P('grp', None, 'brk'), may hold values from -6 to 6
- kappa: float32 [8, 192, 64, 128], P('grp', 'brk'), may hold values from 0.2 to 3
- cut_flags: int32 [8, 192, 64, 128], P('grp', 'brk'), may hold values 0 or 1
- coupling: float32 [5, 5], replicated, may hold values from -2.5 to 2.5
- target: int32 [32, 128], replicated, may hold values from 0 to 4095, as said below
Outputs:
- estimate: float32 [4096, 5, 384], P(('grp', 'brk'))
Inputs may be any that keep to these rules, and one draw needn't show every extreme that they name: `target`: each value owner * 128 + slot appears exactly once; the owner is never in the sender's own level group; a brick sends at most 5 tiles to one owner, and exactly 5 to some owners.
All inputs are finite; a program needn't handle non-finite values. No bound on the sum of `cut_flags` on one device may be relied on, other than what follows from the above.
Results may differ from a plain program's by a relative error of at most 0.00007.
Values sent between devices are 32-bit elements; how exact they have to be, the bound alone decides.
A program may use at most 512 MiB of HBM per device.

v0:
```python
import jax
import jax.numpy as jnp
from jax import lax
from jax.sharding import PartitionSpec as P


def with_halo(x, sides, width):
    for axis, dim in sides:
        size, length = (lax.axis_size(axis), x.shape[dim])
        up = [(i, (i + 1) % size) for i in range(size - 1)]
        down = [(j, i) for i, j in up]
        last = lax.slice_in_dim(x, length - width, length, axis=dim)
        initial = lax.slice_in_dim(x, 0, width, axis=dim)
        before = lax.ppermute(last, axis, up)
        after = lax.ppermute(initial, axis, down)
        x = jnp.concatenate([before, x, after], axis=dim)
    return x


def local(state, adjoint, source, kappa, cut_flags, coupling, target):
    values = state[0]
    fields, cells_x, cells_y, cells_z = values.shape
    framed = with_halo(values, (("brk", 1),), 1)
    framed = jnp.pad(framed, ((0, 0), (0, 0), (1, 1), (1, 1)))
    neighbours = framed[:, 2:, 1:-1, 1:-1] + framed[:, :-2, 1:-1, 1:-1]
    neighbours = neighbours + framed[:, 1:-1, 2:, 1:-1] + framed[:, 1:-1, :-2, 1:-1]
    neighbours = neighbours + framed[:, 1:-1, 1:-1, 2:] + framed[:, 1:-1, 1:-1, :-2]
    coupled = jnp.einsum("fg,gxyz->fxyz", coupling, values, precision=lax.Precision.HIGHEST)
    residual = source[0] - ((6.0 + kappa[0][None]) * values - neighbours + coupled)
    weighted = (1.0 - 0.5 * cut_flags[0].astype(jnp.float32))[None] * adjoint[0] * residual
    groups = lax.axis_size("grp")
    bricks = lax.axis_size("brk")
    owners = groups * bricks
    per_dev = target.shape[1]
    capacity = per_dev // ((groups - 1) * bricks) + 1
    tile_len = cells_x * cells_y * cells_z // 8 // per_dev
    slots_all = owners * capacity
    blocks = weighted.reshape(fields, cells_x // 2, 2, cells_y // 2, 2, cells_z // 2, 2).sum(
        axis=(2, 4, 6)
    )
    pieces = blocks.reshape(fields, per_dev, tile_len)
    myself = lax.axis_index(("grp", "brk"))
    owner_all = target // per_dev
    slot_all = target % per_dev
    tile_rows = lax.broadcasted_iota(jnp.int32, (per_dev, per_dev), 0)
    tile_cols = lax.broadcasted_iota(jnp.int32, (per_dev, per_dev), 1)
    earlier = tile_cols < tile_rows
    same_owner = owner_all[:, :, None] == owner_all[:, None, :]
    rank_all = jnp.sum(jnp.logical_and(same_owner, earlier[None]), axis=2)
    my_owner = lax.dynamic_index_in_dim(owner_all, myself, 0, keepdims=False)
    my_rank = lax.dynamic_index_in_dim(rank_all, myself, 0, keepdims=False)
    send_slot = my_owner * capacity + my_rank
    slot_line = jnp.arange(slots_all, dtype=jnp.int32)
    send_mat = (slot_line[:, None] == send_slot[None, :]).astype(jnp.float32)
    outgoing = jnp.einsum("ot,ftc->foc", send_mat, pieces, precision=lax.Precision.HIGHEST)
    incoming = lax.all_to_all(outgoing, ("grp", "brk"), split_axis=1, concat_axis=1, tiled=True)
    sources = jnp.arange(owners, dtype=jnp.int32)[:, None]
    position = (sources * capacity + rank_all).reshape(-1)
    landing = jnp.where(owner_all == myself, slot_all, per_dev).reshape(-1)
    slot_ids = jnp.arange(per_dev, dtype=jnp.int32)
    matches = landing[None, :] == slot_ids[:, None]
    lookup = jnp.sum(jnp.where(matches, position[None, :], 0), axis=1)
    recv_mat = (lookup[:, None] == slot_line[None, :]).astype(jnp.float32)
    return jnp.einsum("tp,fpc->tfc", recv_mat, incoming, precision=lax.Precision.HIGHEST)


def solution(mesh):
    placed = (
        P("grp", None, "brk", None, None),
        P("grp", None, "brk", None, None),
        P("grp", None, "brk", None, None),
        P("grp", "brk", None, None),
        P("grp", "brk", None, None),
        P(),
        P(),
    )
    return jax.shard_map(
        local, mesh=mesh, in_specs=placed, out_specs=P(("grp", "brk"), None, None), check_vma=False
    )
```

profile of v0, /device:TPU:13, one launch (start us, length us, event | category | flops | bytes accessed | tf_op | source)
XLA Modules:
  0.0 408.0 jit_solution(855887892802374333)
XLA Ops:
  0.0 0.0 copy-start
  0.0 0.0 copy-start.3
  0.0 0.0 copy-start.4
  0.0 0.0 copy-start.10
  0.0 10.7 %copy.35 = f32[1,5,48,64,128]{4,1,3,2,0:T(8,128)S(1)} copy(f32[1,5,48,64,128]{4,3,2,1,0:T(8,128)} %param.7) | data formatting | bytes 15728640 | tf_op args[0]
  10.7 0.0 copy-start.2
  10.7 4.5 %copy-done.2 = f32[1,5,48,64,128]{4,1,3,2,0:T(8,128)} copy-done((f32[1,5,48,64,128]{4,1,3,2,0:T(8,128)}, f32[1,5,48,64,128]{4,1,3,2,0:T(8,128)S(1)}, u32[]{:S(2)}) %copy-start.2) | copy-done | bytes 7864344
  15.2 0.8 fusion.21
  16.0 3.0 collective-permute-start
  19.1 2.4 collective-permute-start.1
  21.6 0.0 copy-done.3
  21.6 0.0 copy-done.4
  21.6 2.0 add_bitcast_fusion
  23.6 0.0 copy-done.10
  23.6 0.6 fusion.17
  24.2 1.3 convert_reduce_fusion
  25.5 0.0 copy-start.7
  25.5 0.6 copy-done.7
  26.1 0.6 add_bitcast_fusion.2
  26.7 0.0 copy-start.5
  26.7 0.0 copy-start.6
  26.7 0.0 collective-permute-done
  26.7 4.2 %collective-permute-done.1 = f32[5,1,64,128]{3,0,2,1:T(8,128)} collective-permute-done((f32[5,1,64,128]{3,0,2,1:T(8,128)}, f32[5,1,64,128]{3,0,2,1:T(8,128)}, u32[]{:S(2)}, u32[]{:S(2)}) %collective-permute-start.1) | collective-permute-done | bytes 163872 | tf_op jit(solution)/shard_map/ppermute | solution.py:14
  31.0 19.3 %select_maximum_fusion = f32[5,50,66,130]{3,0,2,1:T(8,128)} fusion(f32[5,1,64,128]{3,0,2,1:T(8,128)S(1)} %collective-permute-done, f32[5,48,64,128]{3,0,2,1:T(8,128)} %bitcast.38, f32[5,1,64,128]{3,0,2,1:T(8,128)} %collective-permute-done.1), kind=kLoop, calls=%fused_computation.4 | loop fusion | flops 32175000 | bytes 16772000 | tf_op jit(solution)/shard_map/concatenate | solution.py:16
  50.3 0.0 copy-done
  50.3 0.0 copy-done.5
  50.3 0.0 copy-done.6
  50.3 64.2 %fusion.6 = f32[5,48,64,128]{3,0,2,1:T(8,128)} fusion(f32[5,50,66,130]{3,0,2,1:T(8,128)} %select_maximum_fusion, f32[5,48,64,128]{3,0,2,1:T(8,128)} %bitcast.39, f32[5,1,64,128]{3,0,2,1:T(8,128)} %collective-permute-done.1, f32[5,1,64,128]{3,0,2,1:T(8,128)S(1)} %collective-permute-done, f32[1,5,48,64,128]{4,3,2,1,0:T(8,128)} %param.9, ...), kind=kOutput, calls=%fused_computation.13 | convolution fusion | flops 143523840 | bytes 102662240 | tf_op jit(solution)/shard_map/fg,gxyz->fxyz/dot_general | solution.py:28
  114.5 87.6 %copy.25 = f32[5,48,64,128]{0,3,2,1:T(8,128)} copy(f32[5,48,64,128]{3,0,2,1:T(8,128)} %fusion.6) | data formatting | bytes 15728640 | tf_op jit(solution)/shard_map/mul | solution.py:30
  202.2 136.1 %reduce_sum.29 = f32[5,24,32,64]{0,3,2,1:T(8,128)} reduce(f32[5,24,2,32,2,64,2]{0,6,5,4,3,2,1:T(2,128)} %bitcast.10, f32[]{:T(128)} %constant.57.clone.1), dimensions={2,4,6}, to_apply=%region_2.3 | reduce | flops 1720320 | bytes 8847364 | tf_op jit(solution)/shard_map/reduce_sum | solution.py:38
  338.3 0.0 copy-start.1
  338.3 0.0 copy-start.11
  338.3 0.0 copy-start.8
  338.3 0.0 copy-start.9
  338.3 15.1 %copy.26 = f32[5,128,384]{2,1,0:T(8,128)S(1)} copy(f32[5,128,384]{0,2,1:T(8,128)} %bitcast.36) | data formatting | bytes 1966080 | tf_op jit(solution)/shard_map/reshape | solution.py:41
  353.4 0.0 copy-done.11
  353.4 0.7 convolution_bitcast_fusion
  354.1 2.1 copy.27
  356.2 7.2 %all-to-all-start = ((f32[5,160,384]{2,0,1:T(8,128)}), f32[5,160,384]{2,0,1:T(8,128)S(1)}, u32[]{:S(2)}, u32[]{:S(2)}) async-start(f32[5,160,384]{2,0,1:T(8,128)} %copy.27), calls=%async_computation | async-start | bytes 3932160 | tf_op jit(solution)/shard_map/all_to_all | solution.py:56
  363.4 0.0 copy-done.8
  363.4 0.1 add_bitcast_fusion.1
  363.4 0.0 copy-done.9
  363.4 0.3 select_reduce_fusion
  363.8 42.4 %all-to-all-done = f32[5,160,384]{2,0,1:T(8,128)S(1)} async-done(((f32[5,160,384]{2,0,1:T(8,128)}), f32[5,160,384]{2,0,1:T(8,128)S(1)}, u32[]{:S(2)}, u32[]{:S(2)}) %all-to-all-start) | async-done | bytes 1228832 | tf_op jit(solution)/shard_map/all_to_all | solution.py:56
  406.2 1.8 fusion.8
  408.0 0.0 copy-done.1
  (2 shorter events, 0.0 us)
Async XLA Ops:
  0.0 50.3 %copy-start = (f32[5,5]{1,0:T(8,128)S(1)}, f32[5,5]{1,0:T(8,128)}, u32[]{:S(2)}) copy-start(f32[5,5]{1,0:T(8,128)} %param.12) | copy-start | bytes 304
  0.0 21.6 %copy-start.3 = (f32[1,48,64,128]{3,2,1,0:T(8,128)S(1)}, f32[1,48,64,128]{3,2,1,0:T(8,128)}, u32[]{:S(2)}) copy-start(f32[1,48,64,128]{3,2,1,0:T(8,128)} %param.10) | copy-start | bytes 4718596
  0.0 21.6 %copy-start.4 = (s32[1,48,64,128]{3,2,1,0:T(8,128)S(1)}, s32[1,48,64,128]{3,2,1,0:T(8,128)}, u32[]{:S(2)}) copy-start(s32[1,48,64,128]{3,2,1,0:T(8,128)} %param.11) | copy-start | bytes 4718596
  0.0 23.6 %copy-start.10 = (s32[32,128]{1,0:T(8,128)S(1)}, s32[32,128]{1,0:T(8,128)}, u32[]{:S(2)}) copy-start(s32[32,128]{1,0:T(8,128)} %param.13) | copy-start | bytes 49156
  10.7 4.5 %copy-start.2 = (f32[1,5,48,64,128]{4,1,3,2,0:T(8,128)}, f32[1,5,48,64,128]{4,1,3,2,0:T(8,128)S(1)}, u32[]{:S(2)}) copy-start(f32[1,5,48,64,128]{4,1,3,2,0:T(8,128)S(1)} %copy.35) | copy-start | bytes 23592964
  16.0 10.7 %collective-permute-start = (f32[5,1,64,128]{3,0,2,1:T(8,128)}, f32[5,1,64,128]{3,0,2,1:T(8,128)S(1)}, u32[]{:S(2)}, u32[]{:S(2)}) collective-permute-start(f32[5,1,64,128]{3,0,2,1:T(8,128)} %get-tuple-element.6), channel_id=1, source_target_pairs={{1,0},{2,1},{3,2},{5,4},{6,5},{7,6},{9,8},{10,9},{11,10},{13,12},{... | collective-permute-start | bytes 491528 | tf_op jit(solution)/shard_map/ppermute | solution.py:15
  19.1 11.9 %collective-permute-start.1 = (f32[5,1,64,128]{3,0,2,1:T(8,128)}, f32[5,1,64,128]{3,0,2,1:T(8,128)}, u32[]{:S(2)}, u32[]{:S(2)}) collective-permute-start(f32[5,1,64,128]{3,0,2,1:T(8,128)} %get-tuple-element.5), channel_id=1, source_target_pairs={{0,1},{1,2},{2,3},{4,5},{5,6},{6,7},{8,9},{9,10},{10,11},{12,13},{... | collective-permute-start | bytes 491528 | tf_op jit(solution)/shard_map/ppermute | solution.py:14
  25.5 0.6 copy-start.7
  26.7 23.6 %copy-start.5 = (f32[48,64,128]{2,1,0:T(8,128)S(1)}, f32[48,64,128]{2,1,0:T(8,128)}, u32[]{:S(2)}) copy-start(f32[48,64,128]{2,1,0:T(8,128)} %get-tuple-element.9) | copy-start | bytes 4718596
  26.7 23.6 %copy-start.6 = (f32[48,64,128]{2,1,0:T(8,128)S(1)}, f32[48,64,128]{2,1,0:T(8,128)}, u32[]{:S(2)}) copy-start(f32[48,64,128]{2,1,0:T(8,128)} %get-tuple-element.10) | copy-start | bytes 4718596
  338.3 69.7 %copy-start.1 = (f32[5,5]{1,0:T(8,128)S(1)}, f32[5,5]{1,0:T(8,128)}, u32[]{:S(2)}) copy-start(f32[5,5]{1,0:T(8,128)} %param.12) | copy-start | bytes 304
  338.3 15.1 %copy-start.11 = (s32[128]{0:T(128)S(1)}, s32[128]{0:T(128)}, u32[]{:S(2)}) copy-start(s32[128]{0:T(128)} %add_bitcast_fusion.2) | copy-start | bytes 1540
  338.3 25.1 %copy-start.8 = (s32[32,128]{1,0:T(8,128)S(1)}, s32[32,128]{1,0:T(8,128)}, u32[]{:S(2)}) copy-start(s32[32,128]{1,0:T(8,128)} %copy-done.7) | copy-start | bytes 49156
  338.3 25.1 %copy-start.9 = (s32[4096]{0:T(1024)S(1)}, s32[4096]{0:T(1024)}, u32[]{:S(2)}) copy-start(s32[4096]{0:T(1024)} %get-tuple-element.7) | copy-start | bytes 49156
  356.2 50.0 %all-to-all-start = ((f32[5,160,384]{2,0,1:T(8,128)}), f32[5,160,384]{2,0,1:T(8,128)S(1)}, u32[]{:S(2)}, u32[]{:S(2)}) async-start(f32[5,160,384]{2,0,1:T(8,128)} %copy.27), calls=%async_computation | async-start | bytes 3932160 | tf_op jit(solution)/shard_map/all_to_all | solution.py:56
where the time goes:
time: 414 us; the launch traced here: 408 us
  other arithmetic  160 us (39%)
  local copies, waits for them, and re-layouts  121 us (29%)
  matrix products  66.7 us (16%)
  waiting for transfers between devices  46.7 us (11%)
  starting transfers between devices  12.6 us (3%)
    reduce_sum x1, other arithmetic, local(): weighted.reshape(fields, cells_x // 2, 2, cells_y // 2, 2, cells_z // 2, 2)  136 us
    mul x1, local copies, waits for them, and re-layouts, local(): (1.0 - 0.5 * cut_flags[0].astype(jnp.float32))[None] * adjoint[0] * residual  87.6 us
    dot_general x1, matrix products, local(): jnp.einsum('fg,gxyz->fxyz', coupling, values, precision=lax.Precision.HIG...  64.2 us
    all_to_all x1, waiting for transfers between devices, local(): lax.all_to_all(outgoing, ('grp', 'brk'), split_axis=1, concat_axis=1, til...  42.4 us
    concatenate x1, other arithmetic, with_halo(): x = jnp.concatenate([before, x, after], axis=dim)  19.3 us
    unnamed x25, local copies, waits for them, and re-layouts  15.8 us
    reshape x1, local copies, waits for them, and re-layouts, local(): pieces = blocks.reshape(fields, per_dev, tile_len)  15.1 us
  transfers between devices with their start and end apart: 3, of which 2 were waited for; matrix products, arithmetic and copies ran while one was open for 1% of the time, Pallas kernels for 0%

commit v1 on v0

v1 whole, which is shorter than its diff:
```python
import functools
import math

import jax
import jax.numpy as jnp
from jax import lax
from jax.experimental import pallas as pl
from jax.experimental.pallas import tpu as pltpu
from jax.sharding import PartitionSpec as P

F32 = jnp.float32
MESH = pl.DeviceIdType.MESH
PAD = 8
CHUNK = 6


def route_kernel(
    groups, bricks, capacity,
    state, adjoint, source, kappa, flags, coupling, target,
    recv, lookup,
    st, ad, so, ka, fl, acc, packed, outbox, table_v, table_s, slot_v, value_v,
    load_sem, table_sem, halo_send, halo_recv, send_sem, recv_sem,
):
    fields, cells_x, cells_y, lanes = so.shape
    tiles = target.shape[1]
    owners = groups * bricks
    partners = (groups - 1) * bricks
    planes = cells_x // 2
    chunks = cells_x // CHUNK
    per_chunk = CHUNK // 2
    rows = cells_y // 4
    tile_rows = planes * rows // tiles
    grp, brk = lax.axis_index("grp"), lax.axis_index("brk")
    me = grp * bricks + brk

    barrier = pltpu.get_barrier_semaphore()

    def greet(i, carry):
        other = lax.rem(me + i, owners)
        pl.semaphore_signal(
            barrier, inc=1, device_id=(other // bricks, lax.rem(other, bricks)), device_id_type=MESH
        )
        return carry

    def state_load(c):
        return pltpu.make_async_copy(
            state.at[0, :, pl.ds(c * CHUNK, CHUNK)],
            st.at[:, pl.ds(c * CHUNK + 1, CHUNK), pl.ds(PAD, cells_y)],
            load_sem.at[0, c],
        )

    def other_loads(c):
        span = pl.ds(c * CHUNK, CHUNK)
        return (
            pltpu.make_async_copy(adjoint.at[0, :, span], ad.at[:, span], load_sem.at[1, c]),
            pltpu.make_async_copy(source.at[0, :, span], so.at[:, span], load_sem.at[2, c]),
            pltpu.make_async_copy(kappa.at[0, span], ka.at[span], load_sem.at[3, c]),
            pltpu.make_async_copy(flags.at[0, span], fl.at[span], load_sem.at[4, c]),
        )

    state_load(0).start()
    state_load(1).start()
    for c in list(range(1, chunks)) + [0]:
        if 1 <= c < chunks - 1:
            state_load(c + 1).start()
        for copy in other_loads(c):
            copy.start()
    lax.fori_loop(1, owners, greet, 0)

    zeros_pad = jnp.zeros((fields, cells_x + 2, PAD, lanes), F32)
    st[:, :, 0:PAD, :] = zeros_pad
    st[:, :, PAD + cells_y : 2 * PAD + cells_y, :] = zeros_pad
    zeros_face = jnp.zeros((fields, cells_y, lanes), F32)

    @pl.when(brk == 0)
    def _():
        st[:, 0, PAD : PAD + cells_y, :] = zeros_face

    @pl.when(brk == bricks - 1)
    def _():
        st[:, cells_x + 1, PAD : PAD + cells_y, :] = zeros_face

    acc[...] = jnp.zeros_like(acc)

    shift = int(math.log2(tiles))
    earlier = (
        lax.broadcasted_iota(jnp.int32, (tiles, tiles), 0)
        < lax.broadcasted_iota(jnp.int32, (tiles, tiles), 1)
    ).astype(F32).astype(jnp.bfloat16)
    owner_row = lax.broadcasted_iota(jnp.int32, (owners, tiles), 0)
    tile_col = lax.broadcasted_iota(jnp.int32, (owners, tiles), 1)

    def rank_of(chosen):
        return jnp.dot(
            chosen.astype(F32).astype(jnp.bfloat16), earlier, preferred_element_type=F32
        ).astype(jnp.int32)

    mine = lax.shift_right_logical(target[pl.ds(me, 1), :], jnp.int32(shift))
    chosen = jnp.broadcast_to(mine, (owners, tiles)) == owner_row
    rank = rank_of(chosen)
    table = jnp.zeros((owners, tiles), F32)
    for r in range(capacity):
        hit = jnp.logical_and(chosen, rank == r)
        index = jnp.sum(jnp.where(hit, tile_col.astype(F32), 0.0), axis=1, keepdims=True)
        table = jnp.where(tile_col == r, index, table)
    table_v[...] = table.astype(jnp.int32)
    table_copy = pltpu.make_async_copy(table_v, table_s, table_sem)
    table_copy.start()

    coef = [
        [coupling[f, h] + (6.0 if f == h else 0.0) for h in range(fields)] for f in range(fields)
    ]
    lane = lax.broadcasted_iota(jnp.int32, (8, lanes), 1)
    not_first, not_last = lane > 0, lane < lanes - 1
    pair_in = lax.broadcasted_iota(jnp.int32, (2 * lanes, lanes), 0)
    pair_out = lax.broadcasted_iota(jnp.int32, (2 * lanes, lanes), 1)
    pair_sum = (pair_in // 2 == pair_out).astype(F32).astype(jnp.bfloat16)
    count = fields * rows

    def restrict(slot):
        quarter = [acc[slot, pl.ds(q, count, stride=4), :] for q in range(4)]
        both = jnp.concatenate([quarter[0] + quarter[1], quarter[2] + quarter[3]], axis=1)
        high = both.astype(jnp.bfloat16)
        low = (both - high.astype(F32)).astype(jnp.bfloat16)
        return jnp.dot(high, pair_sum, preferred_element_type=F32) + jnp.dot(
            low, pair_sum, preferred_element_type=F32
        )

    def put(plane, result):
        for f in range(fields):
            packed[f, pl.ds(pl.multiple_of(plane * rows, rows), rows), :] = result[
                f * rows : (f + 1) * rows
            ]

    def stencil(plane, slot):
        x = 2 * plane
        for y in range(0, cells_y, 8):
            values = [[st[f, x + i, PAD + y : PAD + y + 8, :] for i in range(4)] for f in range(fields)]
            totals = [None] * fields
            for d in range(2):
                react = ka[x + d, y : y + 8, :]
                weight = 1.0 - 0.5 * fl[x + d, y : y + 8, :].astype(F32)
                for f in range(fields):
                    own = values[f][1 + d]
                    near = values[f][d] + values[f][2 + d]
                    near = near + (
                        st[f, x + 1 + d, PAD + y - 1 : PAD + y + 7, :]
                        + st[f, x + 1 + d, PAD + y + 1 : PAD + y + 9, :]
                    )
                    near = near + (
                        jnp.where(not_first, pltpu.roll(own, 1, 1), 0.0)
                        + jnp.where(not_last, pltpu.roll(own, lanes - 1, 1), 0.0)
                    )
                    mixed = react * own
                    for h in range(fields):
                        mixed = mixed + coef[f][h] * values[h][1 + d]
                    residual = so[f, x + d, y : y + 8, :] - (mixed - near)
                    part = weight * ad[f, x + d, y : y + 8, :] * residual
                    totals[f] = part if d == 0 else totals[f] + part
            for f in range(fields):
                acc[slot, f * cells_y + y : f * cells_y + y + 8, :] = totals[f]

    def step(n, with_state):
        plane = lax.rem(n + per_chunk, planes)
        before = lax.rem(n + per_chunk - 1, planes)

        @pl.when(lax.rem(n, per_chunk) == 0)
        def _():
            c = plane // per_chunk
            if with_state:
                state_load(c + 1).wait()
            for copy in other_loads(c):
                copy.wait()

        result = restrict(lax.rem(n + 1, 2))
        stencil(plane, lax.rem(n, 2))
        put(before, result)

    def steps(start, stop, with_state):
        def body(n, carry):
            step(n, with_state)
            return carry

        lax.fori_loop(start, stop, body, 0)

    state_load(0).wait()
    state_load(1).wait()
    steps(0, per_chunk, True)
    pl.semaphore_wait(barrier, owners - 1)

    inner = pl.ds(PAD, cells_y)
    up = pltpu.make_async_remote_copy(
        src_ref=state.at[0, :, cells_x - 1],
        dst_ref=st.at[:, 0, inner],
        send_sem=halo_send.at[0],
        recv_sem=halo_recv.at[0],
        device_id=(grp, brk + 1),
        device_id_type=MESH,
    )
    down = pltpu.make_async_remote_copy(
        src_ref=state.at[0, :, 0],
        dst_ref=st.at[:, cells_x + 1, inner],
        send_sem=halo_send.at[1],
        recv_sem=halo_recv.at[1],
        device_id=(grp, brk - 1),
        device_id_type=MESH,
    )

    @pl.when(brk < bricks - 1)
    def _():
        up.start()

    @pl.when(brk > 0)
    def _():
        down.start()

    steps(per_chunk, planes - 2 * per_chunk, True)

    @pl.when(brk > 0)
    def _():
        up.wait_recv()
        down.wait_send()

    @pl.when(brk < bricks - 1)
    def _():
        down.wait_recv()
        up.wait_send()

    steps(planes - 2 * per_chunk, planes, False)
    put(per_chunk - 1, restrict((planes - 1) % 2))
    table_copy.wait()

    def outgoing(p):
        ahead = p // bricks + 1
        to_grp, to_brk = lax.rem(grp + ahead, groups), lax.rem(p, bricks)
        place = (ahead - 1) * bricks + brk
        return to_grp * bricks + to_brk, pltpu.make_async_remote_copy(
            src_ref=outbox.at[p],
            dst_ref=recv.at[place],
            send_sem=send_sem.at[p],
            recv_sem=recv_sem.at[place],
            device_id=(to_grp, to_brk),
            device_id_type=MESH,
        )

    def send(p, carry):
        owner, copy = outgoing(p)
        for r in range(capacity):
            t = jnp.clip(table_s[owner, r], 0, tiles - 1)
            for f in range(fields):
                for k in range(tile_rows):
                    outbox[p, (r * fields + f) * tile_rows + k, :, :] = packed[
                        f, pl.ds(t * tile_rows + k, 1), :
                    ]
        copy.start()
        return carry

    lax.fori_loop(0, partners, send, 0)

    every = target[...]
    arriving = lax.shift_right_logical(every, jnp.int32(shift)) == me
    sender_grp = lax.shift_right_logical(owner_row, jnp.int32(int(math.log2(bricks))))
    sender_brk = jnp.bitwise_and(owner_row, bricks - 1)
    ahead = grp - sender_grp
    ahead = jnp.where(ahead < 0, ahead + groups, ahead)
    position = ((ahead - 1) * bricks + sender_brk) * capacity + rank_of(arriving)
    value_v[...] = jnp.where(arriving, position, 0).astype(F32)
    slot_v[...] = jnp.where(arriving, jnp.bitwise_and(every, tiles - 1), -1)
    down_iota = lax.broadcasted_iota(jnp.int32, (tiles, tiles), 0)
    across_iota = lax.broadcasted_iota(jnp.int32, (tiles, tiles), 1)

    def find(s, found):
        slots = jnp.broadcast_to(slot_v[pl.ds(s, 1), :], (tiles, tiles))
        values = jnp.broadcast_to(value_v[pl.ds(s, 1), :], (tiles, tiles))
        return found + jnp.where(slots == down_iota, values, 0.0)

    found = lax.fori_loop(0, owners, find, jnp.zeros((tiles, tiles), F32))
    column = jnp.sum(found, axis=1, keepdims=True)
    line = jnp.sum(jnp.where(down_iota == across_iota, column, 0.0), axis=0, keepdims=True)
    lookup[...] = line.astype(jnp.int32)

    def finish(p, carry):
        _, copy = outgoing(p)
        copy.wait_send()
        pltpu.make_async_remote_copy(
            src_ref=outbox.at[p],
            dst_ref=recv.at[p],
            send_sem=send_sem.at[p],
            recv_sem=recv_sem.at[p],
            device_id=(lax.rem(grp + 1, groups), brk),
            device_id_type=MESH,
        ).wait_recv()
        return carry

    lax.fori_loop(0, partners, finish, 0)


def place_kernel(lookup, received, out, stage):
    fields, tiles, length = out.shape
    lanes = received.shape[-1]
    tile_rows = length // lanes

    def body(i, carry):
        for u in range(8):
            j = i * 8 + u
            base = jnp.clip(lookup[0, j], 0, received.shape[0] // (fields * tile_rows) - 1)
            base = base * (fields * tile_rows)
            for f in range(fields):
                for k in range(tile_rows):
                    stage[f * tile_rows + k, pl.ds(j, 1), :] = received[base + f * tile_rows + k]
        return carry

    lax.fori_loop(0, tiles // 8, body, 0)
    for f in range(fields):
        for k in range(tile_rows):
            out[f, :, k * lanes : (k + 1) * lanes] = stage[f * tile_rows + k]


def local(groups, bricks, state, adjoint, source, kappa, cut_flags, coupling, target):
    _, fields, cells_x, cells_y, lanes = state.shape
    tiles = target.shape[1]
    owners = groups * bricks
    partners = (groups - 1) * bricks
    capacity = tiles // partners + 1
    planes = cells_x // 2
    rows = cells_y // 4
    length = planes * rows * lanes // tiles
    tile_rows = length // lanes
    block = capacity * fields * tile_rows
    chunks = cells_x // CHUNK
    hbm = pl.BlockSpec(memory_space=pl.ANY)
    vmem = pl.BlockSpec(memory_space=pltpu.VMEM)
    smem = pl.BlockSpec(memory_space=pltpu.SMEM)
    brick = (fields, cells_x, cells_y, lanes)
    cells = math.prod(brick)
    received, lookup = pl.pallas_call(
        functools.partial(route_kernel, groups, bricks, capacity),
        out_shape=(
            jax.ShapeDtypeStruct((partners, block, 1, lanes), F32),
            jax.ShapeDtypeStruct((1, tiles), jnp.int32),
        ),
        in_specs=[hbm, hbm, hbm, hbm, hbm, smem, vmem],
        out_specs=(hbm, vmem),
        scratch_shapes=[
            pltpu.VMEM((fields, cells_x + 2, cells_y + 2 * PAD, lanes), F32),
            pltpu.VMEM(brick, F32),
            pltpu.VMEM(brick, F32),
            pltpu.VMEM(brick[1:], F32),
            pltpu.VMEM(brick[1:], jnp.int32),
            pltpu.VMEM((2, fields * cells_y + 8, lanes), F32),
            pltpu.VMEM((fields, planes * rows, lanes), F32),
            pltpu.VMEM((partners, block, 1, lanes), F32),
            pltpu.VMEM((owners, tiles), jnp.int32),
            pltpu.SMEM((owners, tiles), jnp.int32),
            pltpu.VMEM((owners, tiles), jnp.int32),
            pltpu.VMEM((owners, tiles), F32),
            pltpu.SemaphoreType.DMA((5, chunks)),
            pltpu.SemaphoreType.DMA,
            pltpu.SemaphoreType.DMA((2,)),
            pltpu.SemaphoreType.DMA((2,)),
            pltpu.SemaphoreType.DMA((partners,)),
            pltpu.SemaphoreType.DMA((partners,)),
        ],
        compiler_params=pltpu.CompilerParams(
            collective_id=0, has_side_effects=True, vmem_limit_bytes=56 * 1024 * 1024
        ),
        cost_estimate=pl.CostEstimate(flops=25 * cells, bytes_accessed=14 * cells, transcendentals=0),
    )(state, adjoint, source, kappa, cut_flags, coupling, target)
    received = received.reshape(partners * block, 1, lanes)
    placed = pl.pallas_call(
        place_kernel,
        out_shape=jax.ShapeDtypeStruct((fields, tiles, length), F32),
        in_specs=[smem, vmem],
        out_specs=vmem,
        scratch_shapes=[pltpu.VMEM((fields * tile_rows, tiles, lanes), F32)],
        compiler_params=pltpu.CompilerParams(vmem_limit_bytes=24 * 1024 * 1024),
    )(lookup, received)
    return placed.transpose(1, 0, 2)


def solution(mesh):
    placed = (
        P("grp", None, "brk", None, None),
        P("grp", None, "brk", None, None),
        P("grp", None, "brk", None, None),
        P("grp", "brk", None, None),
        P("grp", "brk", None, None),
        P(),
        P(),
    )
    return jax.shard_map(
        functools.partial(local, mesh.shape["grp"], mesh.shape["brk"]),
        mesh=mesh, in_specs=placed, out_specs=P(("grp", "brk"), None, None), check_vma=False,
    )
```

time: 414 us -> 51.1 us (0.12); the launches traced: 408 us -> 50.8 us
  other arithmetic: 160 us -> 0 us
  local copies, waits for them, and re-layouts: 121 us -> 1.89 us
  matrix products: 66.7 us -> 0 us
  Pallas kernels: 0 us -> 48.9 us
  waiting for transfers between devices: 46.7 us -> 0 us
  starting transfers between devices: 12.6 us -> 0 us
    reduce_sum x3 -> x0, other arithmetic: 138 us -> none  [the longest x1 136 us: local(): weighted.reshape(fields, cells_x // 2, 2, cells_y // 2, 2, cells_z // 2, 2)]
    mul x1 -> x0, local copies, waits for them, and re-layouts: 87.6 us -> none  [local(): (1.0 - 0.5 * cut_flags[0].astype(jnp.float32))[None] * adjoint[0] * residual]
    dot_general x3 -> x0, matrix products: 66.7 us -> none  [the longest x1 64.2 us: local(): jnp.einsum('fg,gxyz->fxyz', coupling, values, precision=lax.Precision.HIG...]
    pallas_call x0 -> x2, Pallas kernels: none -> 48.9 us  [the longest x1 46.3 us: local(): pl.pallas_call(functools.partial(route_kernel, groups, bricks, capacity),...]
    all_to_all x1 -> x0, waiting for transfers between devices: 42.4 us -> none  [local(): lax.all_to_all(outgoing, ('grp', 'brk'), split_axis=1, concat_axis=1, til...]
    concatenate x1 -> x0, other arithmetic: 19.3 us -> none  [with_halo(): x = jnp.concatenate([before, x, after], axis=dim)]
    reshape x1 -> x0, local copies, waits for them, and re-layouts: 15.1 us -> none  [local(): pieces = blocks.reshape(fields, per_dev, tile_len)]
    unnamed x25 -> x4, local copies, waits for them, and re-layouts: 15.8 us -> 1.89 us
  transfers between devices with their start and end apart: 3 -> 0, of which waited for: 2 -> 0; matrix products, arithmetic and copies ran while one was open for 1% -> 0% of each run, Pallas kernels for 0% -> 0%
where the time goes in v1:
time: 51.1 us; the launch traced here: 50.8 us
  Pallas kernels  48.9 us (96%)
  local copies, waits for them, and re-layouts  1.89 us (4%)
    pallas_call x1, Pallas kernels, local(): pl.pallas_call(functools.partial(route_kernel, groups, bricks, capacity),...  46.3 us
    pallas_call x1, Pallas kernels, local(): pl.pallas_call(place_kernel, out_shape=jax.ShapeDtypeStruct((fields, tile...  2.62 us
    unnamed x4, local copies, waits for them, and re-layouts  1.89 us

profile of v1, /device:TPU:13, one launch (start us, length us, event | category | flops | bytes accessed | tf_op | source)
XLA Modules:
  0.0 50.8 jit_solution(2255007845219118146)
XLA Ops:
  0.0 46.3 %shard_map.73 = (f32[28,75,1,128]{3,2,1,0:T(1,128)}, s32[1,128]{1,0:T(1,128)}) custom-call(f32[1,5,48,64,128]{4,3,2,1,0:T(8,128)} %state.1, f32[1,5,48,64,128]{4,3,2,1,0:T(8,128)} %adjoint.1, f32[1,5,48,64,128]{4,3,2,1,0:T(8,128)} %source.1, f32[1,48,64,128]{3,2,1,0:T(8,128)} %kappa.1, s32[1,48,64,128]{3,2,1,0:T(8,128)} %flags.1, f32[5,5]{1,0:T(8,128)} %coupling.1, ...), custom_call_target="tpu_custom_call" | custom-call | flops 49152000 | bytes 27525120 | tf_op jit(solution)/shard_map/pallas_call | solution.py:336
  46.3 0.0 copy-start
  46.3 1.2 %copy-done = f32[28,75,1,128]{3,2,1,0:T(1,128)S(1)} copy-done((f32[28,75,1,128]{3,2,1,0:T(1,128)S(1)}, f32[28,75,1,128]{3,2,1,0:T(1,128)}, u32[]{:S(2)}) %copy-start) | copy-done | bytes 1075224
  47.5 0.0 copy-start.1
  47.5 0.7 %copy-done.1 = s32[1,128]{1,0:T(1,128)S(1)} copy-done((s32[1,128]{1,0:T(1,128)S(1)}, s32[1,128]{1,0:T(1,128)}, u32[]{:S(2)}) %copy-start.1) | copy-done | bytes 536
  48.2 2.6 %shard_map.74 = f32[5,128,384]{2,1,0:T(8,128)} custom-call(s32[1,128]{1,0:T(1,128)S(1)} %copy-done.1, f32[2100,1,128]{2,1,0:T(1,128)S(1)} %bitcast.2), custom_call_target="tpu_custom_call" | custom-call | tf_op jit(solution)/shard_map/pallas_call | solution.py:370
Async XLA Ops:
  46.3 1.2 %copy-start = (f32[28,75,1,128]{3,2,1,0:T(1,128)S(1)}, f32[28,75,1,128]{3,2,1,0:T(1,128)}, u32[]{:S(2)}) copy-start(f32[28,75,1,128]{3,2,1,0:T(1,128)} %get-tuple-element.8) | copy-start | bytes 3225604
  47.5 0.7 %copy-start.1 = (s32[1,128]{1,0:T(1,128)S(1)}, s32[1,128]{1,0:T(1,128)}, u32[]{:S(2)}) copy-start(s32[1,128]{1,0:T(1,128)} %get-tuple-element.7.lookup) | copy-start | bytes 1540

commit v2 on v1

v2 whole, which is shorter than its diff:
```python
import functools
import math

import jax
import jax.numpy as jnp
from jax import lax
from jax.experimental import pallas as pl
from jax.experimental.pallas import tpu as pltpu
from jax.sharding import PartitionSpec as P

F32 = jnp.float32
MESH = pl.DeviceIdType.MESH
PAD = 8
CHUNK = 6


def split_fields(fields):
    first = list(range(0, 1))
    rest = list(range(1, fields))
    half = (len(rest) + 1) // 2
    return [part for part in (first, rest[:half], rest[half:]) if part]


def route_kernel(
    groups, bricks, capacity, phases,
    state, adjoint, source, kappa, flags, coupling, target,
    out, *scratch,
):
    stages = len(phases)
    outbox, recv = scratch[:stages], scratch[stages : 2 * stages]
    (
        st, ad, so, ka, fl, acc, packed, table_v, table_s, slot_v, value_v, line_v, line_s, stage,
        load_sem, late_sem, table_sem, line_sem, halo_send, halo_recv, send_sem, recv_sem,
    ) = scratch[2 * stages :]
    fields, cells_x, cells_y, lanes = so.shape
    tiles = target.shape[1]
    owners = groups * bricks
    partners = (groups - 1) * bricks
    planes = cells_x // 2
    chunks = cells_x // CHUNK
    per_chunk = CHUNK // 2
    rows = cells_y // 4
    tile_rows = planes * rows // tiles
    grp, brk = lax.axis_index("grp"), lax.axis_index("brk")
    me = grp * bricks + brk

    barrier = pltpu.get_barrier_semaphore()

    def greet(i, carry):
        other = lax.rem(me + i, owners)
        pl.semaphore_signal(
            barrier, inc=1, device_id=(other // bricks, lax.rem(other, bricks)), device_id_type=MESH
        )
        return carry

    def state_load(c):
        return pltpu.make_async_copy(
            state.at[0, :, pl.ds(c * CHUNK, CHUNK)],
            st.at[:, pl.ds(c * CHUNK + 1, CHUNK), pl.ds(PAD, cells_y)],
            load_sem.at[0, c],
        )

    def other_loads(c):
        span = pl.ds(c * CHUNK, CHUNK)
        here = pl.ds(phases[0][0], len(phases[0]))
        return (
            pltpu.make_async_copy(adjoint.at[0, here, span], ad.at[here, span], load_sem.at[1, c]),
            pltpu.make_async_copy(source.at[0, here, span], so.at[here, span], load_sem.at[2, c]),
            pltpu.make_async_copy(kappa.at[0, span], ka.at[span], load_sem.at[3, c]),
            pltpu.make_async_copy(flags.at[0, span], fl.at[span], load_sem.at[4, c]),
        )

    def late_loads(i):
        here = pl.ds(phases[i][0], len(phases[i]))
        return (
            pltpu.make_async_copy(adjoint.at[0, here], ad.at[here], late_sem.at[0, i]),
            pltpu.make_async_copy(source.at[0, here], so.at[here], late_sem.at[1, i]),
        )

    state_load(0).start()
    state_load(1).start()
    for c in list(range(1, chunks)) + [0]:
        if 1 <= c < chunks - 1:
            state_load(c + 1).start()
        for copy in other_loads(c):
            copy.start()
    for i in range(1, stages):
        for copy in late_loads(i):
            copy.start()
    lax.fori_loop(1, owners, greet, 0)

    zeros_pad = jnp.zeros((fields, cells_x + 2, PAD, lanes), F32)
    st[:, :, 0:PAD, :] = zeros_pad
    st[:, :, PAD + cells_y : 2 * PAD + cells_y, :] = zeros_pad
    zeros_face = jnp.zeros((fields, cells_y, lanes), F32)

    @pl.when(brk == 0)
    def _():
        st[:, 0, PAD : PAD + cells_y, :] = zeros_face

    @pl.when(brk == bricks - 1)
    def _():
        st[:, cells_x + 1, PAD : PAD + cells_y, :] = zeros_face

    acc[...] = jnp.zeros_like(acc)

    shift = int(math.log2(tiles))
    earlier = (
        lax.broadcasted_iota(jnp.int32, (tiles, tiles), 0)
        < lax.broadcasted_iota(jnp.int32, (tiles, tiles), 1)
    ).astype(F32).astype(jnp.bfloat16)
    owner_row = lax.broadcasted_iota(jnp.int32, (owners, tiles), 0)
    tile_col = lax.broadcasted_iota(jnp.int32, (owners, tiles), 1)

    def rank_of(chosen):
        return jnp.dot(
            chosen.astype(F32).astype(jnp.bfloat16), earlier, preferred_element_type=F32
        ).astype(jnp.int32)

    mine = lax.shift_right_logical(target[pl.ds(me, 1), :], jnp.int32(shift))
    chosen = jnp.broadcast_to(mine, (owners, tiles)) == owner_row
    rank = rank_of(chosen)
    table = jnp.zeros((owners, tiles), F32)
    for r in range(capacity):
        hit = jnp.logical_and(chosen, rank == r)
        index = jnp.sum(jnp.where(hit, tile_col.astype(F32), 0.0), axis=1, keepdims=True)
        table = jnp.where(tile_col == r, index, table)
    table_v[...] = table.astype(jnp.int32)
    table_copy = pltpu.make_async_copy(table_v, table_s, table_sem)
    table_copy.start()

    coef = [
        [coupling[f, h] + (6.0 if f == h else 0.0) for h in range(fields)] for f in range(fields)
    ]
    lane = lax.broadcasted_iota(jnp.int32, (8, lanes), 1)
    not_first, not_last = lane > 0, lane < lanes - 1
    pair_in = lax.broadcasted_iota(jnp.int32, (2 * lanes, lanes), 0)
    pair_out = lax.broadcasted_iota(jnp.int32, (2 * lanes, lanes), 1)
    pair_sum = (pair_in // 2 == pair_out).astype(F32).astype(jnp.bfloat16)
    def restrict(slot, fs):
        count = len(fs) * rows
        quarter = [acc[slot, pl.ds(q, count, stride=4), :] for q in range(4)]
        both = jnp.concatenate([quarter[0] + quarter[1], quarter[2] + quarter[3]], axis=1)
        high = both.astype(jnp.bfloat16)
        low = (both - high.astype(F32)).astype(jnp.bfloat16)
        return jnp.dot(high, pair_sum, preferred_element_type=F32) + jnp.dot(
            low, pair_sum, preferred_element_type=F32
        )

    def put(plane, result, fs):
        for i, f in enumerate(fs):
            packed[f, pl.ds(pl.multiple_of(plane * rows, rows), rows), :] = result[
                i * rows : (i + 1) * rows
            ]

    def stencil(plane, slot, fs):
        x = 2 * plane
        for y in range(0, cells_y, 8):
            inside = slice(PAD + y, PAD + y + 8)
            centre = [[st[f, x + 1 + d, inside, :] for d in range(2)] for f in range(fields)]
            totals = [None] * len(fs)
            for d in range(2):
                react = ka[x + d, y : y + 8, :]
                weight = 1.0 - 0.5 * fl[x + d, y : y + 8, :].astype(F32)
                for i, f in enumerate(fs):
                    own = centre[f][d]
                    near = centre[f][1 - d] + st[f, x + 3 * d, inside, :]
                    near = near + (
                        st[f, x + 1 + d, PAD + y - 1 : PAD + y + 7, :]
                        + st[f, x + 1 + d, PAD + y + 1 : PAD + y + 9, :]
                    )
                    near = near + (
                        jnp.where(not_first, pltpu.roll(own, 1, 1), 0.0)
                        + jnp.where(not_last, pltpu.roll(own, lanes - 1, 1), 0.0)
                    )
                    mixed = react * own
                    for h in range(fields):
                        mixed = mixed + coef[f][h] * centre[h][d]
                    residual = so[f, x + d, y : y + 8, :] - (mixed - near)
                    part = weight * ad[f, x + d, y : y + 8, :] * residual
                    totals[i] = part if d == 0 else totals[i] + part
            for i in range(len(fs)):
                acc[slot, i * cells_y + y : i * cells_y + y + 8, :] = totals[i]

    def steps(start, stop, fs, with_loads, with_state):
        def body(n, carry):
            plane = lax.rem(n + per_chunk, planes)
            before = lax.rem(n + per_chunk - 1, planes)
            if with_loads:

                @pl.when(lax.rem(n, per_chunk) == 0)
                def _():
                    c = plane // per_chunk
                    if with_state:
                        state_load(c + 1).wait()
                    for copy in other_loads(c):
                        copy.wait()

            result = restrict(lax.rem(n + 1, 2), fs)
            stencil(plane, lax.rem(n, 2), fs)
            put(before, result, fs)
            return carry

        lax.fori_loop(start, stop, body, 0)

    inner = pl.ds(PAD, cells_y)

    def faces(i):
        here = pl.ds(phases[i][0], len(phases[i]))
        up = pltpu.make_async_remote_copy(
            src_ref=state.at[0, here, cells_x - 1],
            dst_ref=st.at[here, 0, inner],
            send_sem=halo_send.at[0, i],
            recv_sem=halo_recv.at[0, i],
            device_id=(grp, brk + 1),
            device_id_type=MESH,
        )
        down = pltpu.make_async_remote_copy(
            src_ref=state.at[0, here, 0],
            dst_ref=st.at[here, cells_x + 1, inner],
            send_sem=halo_send.at[1, i],
            recv_sem=halo_recv.at[1, i],
            device_id=(grp, brk - 1),
            device_id_type=MESH,
        )
        return up, down

    def start_faces():
        for i in range(stages):
            up, down = faces(i)

            @pl.when(brk < bricks - 1)
            def _():
                up.start()

            @pl.when(brk > 0)
            def _():
                down.start()

    def wait_faces(i):
        up, down = faces(i)

        @pl.when(brk > 0)
        def _():
            up.wait_recv()
            down.wait_send()

        @pl.when(brk < bricks - 1)
        def _():
            down.wait_recv()
            up.wait_send()

    def outgoing(i, p):
        ahead = p // bricks + 1
        to_grp, to_brk = lax.rem(grp + ahead, groups), lax.rem(p, bricks)
        place = (ahead - 1) * bricks + brk
        return to_grp * bricks + to_brk, pltpu.make_async_remote_copy(
            src_ref=outbox[i].at[p],
            dst_ref=recv[i].at[place],
            send_sem=send_sem.at[i, p],
            recv_sem=recv_sem.at[i, place],
            device_id=(to_grp, to_brk),
            device_id_type=MESH,
        )

    def send_all(i, fs):
        def send(p, carry):
            owner, copy = outgoing(i, p)
            for r in range(capacity):
                t = jnp.clip(table_s[owner, r], 0, tiles - 1) * tile_rows
                for j, f in enumerate(fs):
                    for k in range(tile_rows):
                        outbox[i][p, (r * len(fs) + j) * tile_rows + k, :, :] = packed[
                            f, pl.ds(t + k, 1), :
                        ]
            copy.start()
            return carry

        lax.fori_loop(0, partners, send, 0)

    for i, fs in enumerate(phases):
        if i == 0:
            state_load(0).wait()
            state_load(1).wait()
            steps(0, per_chunk, fs, True, True)
            pl.semaphore_wait(barrier, owners - 1)
            start_faces()
            steps(per_chunk, planes - 2 * per_chunk, fs, True, True)
            wait_faces(0)
            steps(planes - 2 * per_chunk, planes, fs, True, False)
            table_copy.wait()
        else:
            for copy in late_loads(i):
                copy.wait()
            wait_faces(i)
            steps(0, planes, fs, False, False)
        put(per_chunk - 1, restrict((planes - 1) % 2, fs), fs)
        send_all(i, fs)

    every = target[...]
    arriving = lax.shift_right_logical(every, jnp.int32(shift)) == me
    sender_grp = lax.shift_right_logical(owner_row, jnp.int32(int(math.log2(bricks))))
    sender_brk = jnp.bitwise_and(owner_row, bricks - 1)
    ahead = grp - sender_grp
    ahead = jnp.where(ahead < 0, ahead + groups, ahead)
    position = ((ahead - 1) * bricks + sender_brk) * capacity + rank_of(arriving)
    value_v[...] = jnp.where(arriving, position, 0).astype(F32)
    slot_v[...] = jnp.where(arriving, jnp.bitwise_and(every, tiles - 1), -1)
    down_iota = lax.broadcasted_iota(jnp.int32, (tiles, tiles), 0)
    across_iota = lax.broadcasted_iota(jnp.int32, (tiles, tiles), 1)

    def find(s, found):
        slots = jnp.broadcast_to(slot_v[pl.ds(s, 1), :], (tiles, tiles))
        values = jnp.broadcast_to(value_v[pl.ds(s, 1), :], (tiles, tiles))
        return found + jnp.where(slots == down_iota, values, 0.0)

    found = lax.fori_loop(0, owners, find, jnp.zeros((tiles, tiles), F32))
    column = jnp.sum(found, axis=1, keepdims=True)
    line = jnp.sum(jnp.where(down_iota == across_iota, column, 0.0), axis=0, keepdims=True)
    line_v[...] = line.astype(jnp.int32)
    line_copy = pltpu.make_async_copy(line_v, line_s, line_sem)
    line_copy.start()
    line_copy.wait()

    for i, fs in enumerate(phases):

        def arrive(p, carry):
            pltpu.make_async_remote_copy(
                src_ref=outbox[i].at[p],
                dst_ref=recv[i].at[p],
                send_sem=send_sem.at[i, p],
                recv_sem=recv_sem.at[i, p],
                device_id=(lax.rem(grp + 1, groups), brk),
                device_id_type=MESH,
            ).wait_recv()
            return carry

        lax.fori_loop(0, partners, arrive, 0)
        block = len(fs) * tile_rows

        def place_tiles(n, carry):
            for u in range(8):
                slot = n * 8 + u
                at = jnp.clip(line_s[0, slot], 0, partners * capacity - 1)
                box, first = at // capacity, lax.rem(at, capacity) * block
                for j in range(block):
                    stage[j, pl.ds(slot, 1), :] = recv[i][box, first + j, :, :]
            return carry

        lax.fori_loop(0, tiles // 8, place_tiles, 0)
        for j, f in enumerate(fs):
            for k in range(tile_rows):
                out[f, :, k * lanes : (k + 1) * lanes] = stage[j * tile_rows + k]

    for i in range(stages):

        def sent(p, carry):
            outgoing(i, p)[1].wait_send()
            return carry

        lax.fori_loop(0, partners, sent, 0)


def local(groups, bricks, state, adjoint, source, kappa, cut_flags, coupling, target):
    _, fields, cells_x, cells_y, lanes = state.shape
    tiles = target.shape[1]
    owners = groups * bricks
    partners = (groups - 1) * bricks
    capacity = tiles // partners + 1
    planes = cells_x // 2
    rows = cells_y // 4
    length = planes * rows * lanes // tiles
    tile_rows = length // lanes
    chunks = cells_x // CHUNK
    phases = split_fields(fields)
    stages = len(phases)
    widest = max(len(fs) for fs in phases)
    hbm = pl.BlockSpec(memory_space=pl.ANY)
    vmem = pl.BlockSpec(memory_space=pltpu.VMEM)
    smem = pl.BlockSpec(memory_space=pltpu.SMEM)
    brick = (fields, cells_x, cells_y, lanes)
    cells = math.prod(brick)
    boxes = [
        pltpu.VMEM((partners, capacity * len(fs) * tile_rows, 1, lanes), F32) for fs in phases
    ]
    placed = pl.pallas_call(
        functools.partial(route_kernel, groups, bricks, capacity, phases),
        out_shape=jax.ShapeDtypeStruct((fields, tiles, length), F32),
        in_specs=[hbm, hbm, hbm, hbm, hbm, smem, vmem],
        out_specs=vmem,
        scratch_shapes=boxes + boxes + [
            pltpu.VMEM((fields, cells_x + 2, cells_y + 2 * PAD, lanes), F32),
            pltpu.VMEM(brick, F32),
            pltpu.VMEM(brick, F32),
            pltpu.VMEM(brick[1:], F32),
            pltpu.VMEM(brick[1:], jnp.int32),
            pltpu.VMEM((2, widest * cells_y + 8, lanes), F32),
            pltpu.VMEM((fields, planes * rows, lanes), F32),
            pltpu.VMEM((owners, tiles), jnp.int32),
            pltpu.SMEM((owners, tiles), jnp.int32),
            pltpu.VMEM((owners, tiles), jnp.int32),
            pltpu.VMEM((owners, tiles), F32),
            pltpu.VMEM((1, tiles), jnp.int32),
            pltpu.SMEM((1, tiles), jnp.int32),
            pltpu.VMEM((widest * tile_rows, tiles, lanes), F32),
            pltpu.SemaphoreType.DMA((5, chunks)),
            pltpu.SemaphoreType.DMA((2, stages)),
            pltpu.SemaphoreType.DMA,
            pltpu.SemaphoreType.DMA,
            pltpu.SemaphoreType.DMA((2, stages)),
            pltpu.SemaphoreType.DMA((2, stages)),
            pltpu.SemaphoreType.DMA((stages, partners)),
            pltpu.SemaphoreType.DMA((stages, partners)),
        ],
        compiler_params=pltpu.CompilerParams(
            collective_id=0, has_side_effects=True, vmem_limit_bytes=56 * 1024 * 1024
        ),
        cost_estimate=pl.CostEstimate(flops=25 * cells, bytes_accessed=14 * cells, transcendentals=0),
    )(state, adjoint, source, kappa, cut_flags, coupling, target)
    return placed.transpose(1, 0, 2)


def solution(mesh):
    placed = (
        P("grp", None, "brk", None, None),
        P("grp", None, "brk", None, None),
        P("grp", None, "brk", None, None),
        P("grp", "brk", None, None),
        P("grp", "brk", None, None),
        P(),
        P(),
    )
    return jax.shard_map(
        functools.partial(local, mesh.shape["grp"], mesh.shape["brk"]),
        mesh=mesh, in_specs=placed, out_specs=P(("grp", "brk"), None, None), check_vma=False,
    )
```

time: 51.1 us -> 46.5 us (0.910)
  Pallas kernels: 48.9 us -> 43.8 us
    pallas_call x2 -> x1, Pallas kernels: 48.9 us -> 43.8 us  [local(): pl.pallas_call(functools.partial(route_kernel, groups, bricks, capacity,...]
    unnamed x4 -> x1, local copies, waits for them, and re-layouts: 1.89 us -> 2.21 us
where the time goes in v2:
time: 46.5 us; the launch traced here: 46 us
  Pallas kernels  43.8 us (94%)
  local copies, waits for them, and re-layouts  2.21 us (5%)
    pallas_call x1, Pallas kernels, local(): pl.pallas_call(functools.partial(route_kernel, groups, bricks, capacity,...  43.8 us
    unnamed x1, local copies, waits for them, and re-layouts  2.21 us

profile of v2, /device:TPU:13, one launch (start us, length us, event | category | flops | bytes accessed | tf_op | source)
XLA Modules:
  0.0 46.0 jit_solution(8858887155365695778)
XLA Ops:
  0.0 43.8 %shard_map.73 = f32[5,128,384]{2,1,0:T(8,128)} custom-call(f32[1,5,48,64,128]{4,3,2,1,0:T(8,128)} %state.1, f32[1,5,48,64,128]{4,3,2,1,0:T(8,128)} %adjoint.1, f32[1,5,48,64,128]{4,3,2,1,0:T(8,128)} %source.1, f32[1,48,64,128]{3,2,1,0:T(8,128)} %kappa.1, s32[1,48,64,128]{3,2,1,0:T(8,128)} %flags.1, f32[5,5]{1,0:T(8,128)} %coupling.1, s32[32,128]{1,0:T(8,128)} %target.1), custom_call_target="tpu_custom_call" | custom-call | flops 49152000 | bytes 27525120 | tf_op jit(solution)/shard_map/pallas_call | solution.py:386
  43.8 2.2 %copy.9 = f32[128,5,384]{2,0,1:T(8,128)} copy(f32[128,5,384]{2,0,1:T(8,128)} %bitcast.1) | data formatting | bytes 1966080

commit v3 on v2

--- a/solution.py
+++ b/solution.py
@@ -102,8 +102,6 @@
     def _():
         st[:, cells_x + 1, PAD : PAD + cells_y, :] = zeros_face
 
-    acc[...] = jnp.zeros_like(acc)
-
     shift = int(math.log2(tiles))
     earlier = (
         lax.broadcasted_iota(jnp.int32, (tiles, tiles), 0)
@@ -134,26 +132,34 @@
     ]
     lane = lax.broadcasted_iota(jnp.int32, (8, lanes), 1)
     not_first, not_last = lane > 0, lane < lanes - 1
-    pair_in = lax.broadcasted_iota(jnp.int32, (2 * lanes, lanes), 0)
-    pair_out = lax.broadcasted_iota(jnp.int32, (2 * lanes, lanes), 1)
-    pair_sum = (pair_in // 2 == pair_out).astype(F32).astype(jnp.bfloat16)
-    def restrict(slot, fs):
+    most = max(len(fs) for fs in phases) * rows
+    spot = lax.broadcasted_iota(jnp.int32, (most, lanes), 1)
+    even_lane = jnp.bitwise_and(spot, 1) == 0
+    half = lanes // 2
+    order = jnp.where(spot < half, 2 * spot, 2 * (spot - half) + 1)
+
+    def restrict(plane, fs):
         count = len(fs) * rows
-        quarter = [acc[slot, pl.ds(q, count, stride=4), :] for q in range(4)]
-        both = jnp.concatenate([quarter[0] + quarter[1], quarter[2] + quarter[3]], axis=1)
-        high = both.astype(jnp.bfloat16)
-        low = (both - high.astype(F32)).astype(jnp.bfloat16)
-        return jnp.dot(high, pair_sum, preferred_element_type=F32) + jnp.dot(
-            low, pair_sum, preferred_element_type=F32
-        )
-
-    def put(plane, result, fs):
+        quarter = [acc[plane, pl.ds(q, count, stride=4), :] for q in range(4)]
+        first, second = quarter[0] + quarter[1], quarter[2] + quarter[3]
+        first = first + pltpu.roll(first, lanes - 1, 1)
+        second = second + pltpu.roll(second, 1, 1)
+        mixed = jnp.where(even_lane[:count], first, second)
+        result = jnp.take_along_axis(mixed, order[:count], axis=1, mode="promise_in_bounds")
         for i, f in enumerate(fs):
             packed[f, pl.ds(pl.multiple_of(plane * rows, rows), rows), :] = result[
                 i * rows : (i + 1) * rows
             ]
 
-    def stencil(plane, slot, fs):
+    def restrict_all(fs):
+        def body(n, carry):
+            for u in range(4):
+                restrict(n * 4 + u, fs)
+            return carry
+
+        lax.fori_loop(0, planes // 4, body, 0)
+
+    def stencil(plane, fs):
         x = 2 * plane
         for y in range(0, cells_y, 8):
             inside = slice(PAD + y, PAD + y + 8)
@@ -180,25 +186,18 @@
                     part = weight * ad[f, x + d, y : y + 8, :] * residual
                     totals[i] = part if d == 0 else totals[i] + part
             for i in range(len(fs)):
-                acc[slot, i * cells_y + y : i * cells_y + y + 8, :] = totals[i]
+                acc[plane, i * cells_y + y : i * cells_y + y + 8, :] = totals[i]
 
     def steps(start, stop, fs, with_loads, with_state):
         def body(n, carry):
-            plane = lax.rem(n + per_chunk, planes)
-            before = lax.rem(n + per_chunk - 1, planes)
+            c = lax.rem(n + 1, chunks)
             if with_loads:
-
-                @pl.when(lax.rem(n, per_chunk) == 0)
-                def _():
-                    c = plane // per_chunk
-                    if with_state:
-                        state_load(c + 1).wait()
-                    for copy in other_loads(c):
-                        copy.wait()
-
-            result = restrict(lax.rem(n + 1, 2), fs)
-            stencil(plane, lax.rem(n, 2), fs)
-            put(before, result, fs)
+                if with_state:
+                    state_load(c + 1).wait()
+                for copy in other_loads(c):
+                    copy.wait()
+            for u in range(per_chunk):
+                stencil(c * per_chunk + u, fs)
             return carry
 
         lax.fori_loop(start, stop, body, 0)
@@ -282,19 +281,19 @@
         if i == 0:
             state_load(0).wait()
             state_load(1).wait()
-            steps(0, per_chunk, fs, True, True)
+            steps(0, 1, fs, True, True)
             pl.semaphore_wait(barrier, owners - 1)
             start_faces()
-            steps(per_chunk, planes - 2 * per_chunk, fs, True, True)
+            steps(1, chunks - 2, fs, True, True)
             wait_faces(0)
-            steps(planes - 2 * per_chunk, planes, fs, True, False)
+            steps(chunks - 2, chunks, fs, True, False)
             table_copy.wait()
         else:
             for copy in late_loads(i):
                 copy.wait()
             wait_faces(i)
-            steps(0, planes, fs, False, False)
-        put(per_chunk - 1, restrict((planes - 1) % 2, fs), fs)
+            steps(0, chunks, fs, False, False)
+        restrict_all(fs)
         send_all(i, fs)
 
     every = target[...]
@@ -394,7 +393,7 @@
             pltpu.VMEM(brick, F32),
             pltpu.VMEM(brick[1:], F32),
             pltpu.VMEM(brick[1:], jnp.int32),
-            pltpu.VMEM((2, widest * cells_y + 8, lanes), F32),
+            pltpu.VMEM((planes, widest * cells_y + 8, lanes), F32),
             pltpu.VMEM((fields, planes * rows, lanes), F32),
             pltpu.VMEM((owners, tiles), jnp.int32),
             pltpu.SMEM((owners, tiles), jnp.int32),

time: 46.5 us -> 47 us (1.011)
  no operation moved by 1% of the time
where the time goes in v3:
time: 47 us; the launch traced here: 46.3 us
  Pallas kernels  44 us (94%)
  local copies, waits for them, and re-layouts  2.21 us (5%)
    pallas_call x1, Pallas kernels, local(): pl.pallas_call(functools.partial(route_kernel, groups, bricks, capacity,...  44 us
    unnamed x1, local copies, waits for them, and re-layouts  2.21 us

profile of v3, /device:TPU:13, one launch (start us, length us, event | category | flops | bytes accessed | tf_op | source)
XLA Modules:
  0.0 46.3 jit_solution(16665224063291703953)
XLA Ops:
  0.0 44.0 %shard_map.73 = f32[5,128,384]{2,1,0:T(8,128)} custom-call(f32[1,5,48,64,128]{4,3,2,1,0:T(8,128)} %state.1, f32[1,5,48,64,128]{4,3,2,1,0:T(8,128)} %adjoint.1, f32[1,5,48,64,128]{4,3,2,1,0:T(8,128)} %source.1, f32[1,48,64,128]{3,2,1,0:T(8,128)} %kappa.1, s32[1,48,64,128]{3,2,1,0:T(8,128)} %flags.1, f32[5,5]{1,0:T(8,128)} %coupling.1, s32[32,128]{1,0:T(8,128)} %target.1), custom_call_target="tpu_custom_call" | custom-call | flops 49152000 | bytes 27525120 | tf_op jit(solution)/shard_map/pallas_call | solution.py:385
  44.0 2.2 %copy.9 = f32[128,5,384]{2,0,1:T(8,128)} copy(f32[128,5,384]{2,0,1:T(8,128)} %bitcast.1) | data formatting | bytes 1966080

commit v4 on v3

--- a/solution.py
+++ b/solution.py
@@ -250,8 +250,8 @@
             up.wait_send()
 
     def outgoing(i, p):
-        ahead = p // bricks + 1
-        to_grp, to_brk = lax.rem(grp + ahead, groups), lax.rem(p, bricks)
+        ahead = lax.rem(p + brk, groups - 1) + 1
+        to_grp, to_brk = lax.rem(grp + ahead, groups), lax.rem(brk + p // (groups - 1), bricks)
         place = (ahead - 1) * bricks + brk
         return to_grp * bricks + to_brk, pltpu.make_async_remote_copy(
             src_ref=outbox[i].at[p],

time: 47 us -> 48.5 us (1.032)
  the two profiles are of different devices: /device:TPU:13 before, /device:TPU:0 now
where the time goes in v4:
time: 48.5 us; the launch traced here: 48.2 us
  Pallas kernels  46 us (95%)
  local copies, waits for them, and re-layouts  2.21 us (5%)
    pallas_call x1, Pallas kernels, local(): pl.pallas_call(functools.partial(route_kernel, groups, bricks, capacity,...  46 us
    unnamed x1, local copies, waits for them, and re-layouts  2.21 us

profile of v4, /device:TPU:0, one launch (start us, length us, event | category | flops | bytes accessed | tf_op | source)
XLA Modules:
  0.0 48.2 jit_solution(16507291534648289553)
XLA Ops:
  0.0 46.0 %shard_map.73 = f32[5,128,384]{2,1,0:T(8,128)} custom-call(f32[1,5,48,64,128]{4,3,2,1,0:T(8,128)} %state.1, f32[1,5,48,64,128]{4,3,2,1,0:T(8,128)} %adjoint.1, f32[1,5,48,64,128]{4,3,2,1,0:T(8,128)} %source.1, f32[1,48,64,128]{3,2,1,0:T(8,128)} %kappa.1, s32[1,48,64,128]{3,2,1,0:T(8,128)} %flags.1, f32[5,5]{1,0:T(8,128)} %coupling.1, s32[32,128]{1,0:T(8,128)} %target.1), custom_call_target="tpu_custom_call" | custom-call | flops 49152000 | bytes 27525120 | tf_op jit(solution)/shard_map/pallas_call | solution.py:385
  46.0 2.2 %copy.9 = f32[128,5,384]{2,0,1:T(8,128)} copy(f32[128,5,384]{2,0,1:T(8,128)} %bitcast.1) | data formatting | bytes 1966080
